TPU v7x, 256 devices: a whole 4x4x8 slice. The times are simulated.
256 devices in a mesh: space: 32 (over z, y), group: 8 (over x, core).
Axes of the slice: x: 4, y: 4, z: 8, core: 2. Of those that a mesh axis runs over, the one named last changes fastest.
Arguments:
- feats: bfloat16 [8, 262144, 128], P('group', 'space'), may hold values from -6 to 6
- geom: bfloat16 [8, 262144, 128], P('group', 'space'), may hold values from -6 to 6
- w_value: bfloat16 [128, 128], replicated, may hold values from -0.5 to 0.5
- w_kern: bfloat16 [128, 64], replicated, may hold values from -0.5 to 0.5
- w_out: bfloat16 [128, 128], replicated, may hold values from -0.5 to 0.5
- gain: float32 [128], replicated, may hold values from 0.1 to 1.9
- t_local: int32 [8, 2048], P('group', 'space'), may hold values from 0 to 31
- t_dest: int32 [8, 2048, 1], P('group', 'space'), may hold values from 0 to 31; in each aligned block of 64 rows (0 to 63, 64 to 127, ..., all dimensions but the last counted through in order) at most 3 rows name the same one
- t_block: int32 [8, 2048], P('group', 'space'), may hold values from 0 to 31
- t_cut: int32 [8, 2048], P('group', 'space'), may hold values from 64 to 511
- x_local: int32 [8, 256], P('group', 'space'), may hold values from 0 to 31
- x_block: int32 [8, 256], P('group', 'space'), may hold values from 0 to 31
- x_cut: int32 [8, 256], P('group', 'space'), may hold values from 64 to 511
Outputs:
- mixed: bfloat16 [8, 262144, 128], P('group', 'space')
Inputs may be any that keep to these rules, and one draw needn't show every extreme that they name: `t_dest`: among the 64 pairs of one device, no index is named by more than 3 pairs, a bound that some block reaches.
All inputs are finite; a program needn't handle non-finite values.
Results may differ from a plain program's by a relative error of at most 0.0054.
Values may be sent and summed in bfloat16 or wider, within the bound.
No kernel may reach another device: no remote copies, remote signals or barrier semaphores. Data moves between devices by JAX's collectives and lax.ppermute only.
A program may use at most 192 MiB of HBM per device.

v0:
```python
import math

import jax
import jax.numpy as jnp
from jax import lax
from jax.sharding import PartitionSpec as P

C = 128
K = 64
BLK = 256


def from_behind(value, axis, steps):
    count = lax.axis_size(axis)
    leading, last = (max(0, -steps), min(count, count - steps))
    return lax.ppermute(value, axis, [(source, source + steps) for source in range(leading, last)])


def kernel_matrix(left_kern, right_kern, cutoff):
    scores = jnp.dot(left_kern, right_kern.T, preferred_element_type=jnp.float32)
    places = jnp.arange(BLK, dtype=jnp.int32)
    inside = places[:, None] + places[None, :] < cutoff
    return jnp.where(inside, jnp.tanh(scores * (1.0 / math.sqrt(K))), 0.0).astype(jnp.bfloat16)


def both_terms(left_block, right_block, cutoff):
    matrix = kernel_matrix(left_block[:, C:], right_block[:, C:], cutoff)
    forward = jnp.dot(matrix, right_block[:, :C], preferred_element_type=jnp.float32)
    backward = jnp.dot(matrix.T, left_block[:, :C], preferred_element_type=jnp.float32)
    return (forward, backward)


def blockwise(handler, lefts, rights, cutoffs):
    number = lefts.shape[0]
    width = math.gcd(number, 8)

    def evaluate(items):
        return jax.vmap(handler)(items[0], items[1], items[2])

    shaped = tuple(
        (
            stacked.reshape((number // width, width) + stacked.shape[1:])
            for stacked in (lefts, rights, cutoffs)
        )
    )
    result = lax.map(evaluate, shaped)
    return jax.tree.map(lambda stacked: stacked.reshape((number,) + stacked.shape[2:]), result)


def body(
    feats,
    geom,
    w_value,
    w_kern,
    w_out,
    gain,
    t_local,
    t_dest,
    t_block,
    t_cut,
    x_local,
    x_block,
    x_cut,
):
    points = feats[0]
    blocks = points.shape[0] // BLK
    values = jnp.dot(points, w_value, preferred_element_type=jnp.float32).astype(jnp.bfloat16)
    kernels = jnp.dot(geom[0], w_kern, preferred_element_type=jnp.float32).astype(jnp.bfloat16)
    payload = jnp.concatenate([values, kernels], 1).reshape(blocks, BLK, C + K)
    local_ids = t_local[0]
    target = t_dest[0, :, 0]
    partner_ids = t_block[0]
    cutoffs = t_cut[0]
    tiles_here = local_ids.shape[0]
    space_size = lax.axis_size("space")
    capacity = max(3, (3 * tiles_here + 2 * space_size - 1) // (2 * space_size))
    slots = space_size * capacity
    order = jnp.arange(tiles_here, dtype=jnp.int32)
    earlier = (target[:, None] == target[None, :]) & (order[None, :] < order[:, None])
    slot_index = target * capacity + jnp.sum(earlier, 1)
    asked = jnp.zeros((slots,), jnp.int32).at[slot_index].set(partner_ids)
    own_blocks = payload[local_ids]
    aggregate = jnp.zeros((blocks, BLK, C), jnp.float32)
    requested = lax.all_to_all(asked, "space", split_axis=0, concat_axis=0, tiled=True)
    served = payload[requested]
    replies = lax.all_to_all(served, "space", split_axis=0, concat_axis=0, tiled=True)
    partners = replies[slot_index]
    forward, backward = blockwise(both_terms, own_blocks, partners, cutoffs)
    aggregate = aggregate.at[local_ids].add(forward)
    returned = jnp.zeros((slots, BLK, C), jnp.float32).at[slot_index].set(backward)
    received = lax.all_to_all(returned, "space", split_axis=0, concat_axis=0, tiled=True)
    aggregate = aggregate.at[requested].add(received)
    cross_mine = x_local[0]
    cross_theirs = x_block[0]
    upper_side = from_behind(payload, "group", -1)
    forward_x, backward_x = blockwise(
        both_terms, payload[cross_mine], upper_side[cross_theirs], x_cut[0]
    )
    aggregate = aggregate.at[cross_mine].add(forward_x)
    lowered = jnp.zeros((blocks, BLK, C), jnp.float32).at[cross_theirs].add(backward_x)
    aggregate = aggregate + from_behind(lowered.astype(jnp.bfloat16), "group", 1).astype(
        lowered.dtype
    )
    flat = aggregate.reshape(-1, C)
    meansq = jnp.mean(flat * flat, -1, keepdims=True)
    normed = flat * lax.rsqrt(meansq + 1e-06) * gain
    hidden = jax.nn.gelu(normed).astype(jnp.bfloat16)
    mixed = points.astype(jnp.float32) + jnp.dot(hidden, w_out, preferred_element_type=jnp.float32)
    return mixed.astype(jnp.bfloat16)[None]


def solution(mesh):
    in_specs = (
        P("group", "space", None),
        P("group", "space", None),
        P(),
        P(),
        P(),
        P(),
        P("group", "space"),
        P("group", "space", None),
        P("group", "space"),
        P("group", "space"),
        P("group", "space"),
        P("group", "space"),
        P("group", "space"),
    )
    out_specs = P("group", "space", None)
    return jax.shard_map(body, mesh=mesh, in_specs=in_specs, out_specs=out_specs, check_vma=False)
```

profile of v0, /device:TPU:42, one launch (start us, length us, event | category | flops | bytes accessed | tf_op | source)
XLA Modules:
  0.0 658.7 jit_solution(5935683293948214232)
XLA Ops:
  3.3 11.2 %all-to-all-start = ((s32[32,3,1]{1,2,0:T(1,128)}), s32[32,3,1]{1,2,0:T(1,128)S(1)}, u32[]{:S(2)}, u32[]{:S(2)}) async-start(s32[32,3,1]{1,2,0:T(1,128)} %bitcast.20), calls=%async_computation | async-start | bytes 32768 | tf_op jit(solution)/shard_map/all_to_all | solution.py:84
  14.5 2.3 convolution_convert_fusion
  18.1 2.0 copy.63
  20.1 2.0 all-to-all-done
  23.5 9.4 %gather_fusion.3 = bf16[96,256,192]{1,2,0:T(8,128)(2,1)} fusion(bf16[32,256,192]{1,2,0:T(8,128)(2,1)} %bitcast.87, s32[1024]{0:T(1024)S(1)} %pad_clamp_fusion.1), kind=kCustom, calls=%fused_computation.3 | custom fusion | bytes 18874752 | tf_op jit(solution)/shard_map/gather | solution.py:85
  32.9 8.0 %all-to-all-start.1 = ((bf16[96,256,192]{1,2,0:T(8,128)(2,1)}), bf16[96,256,192]{1,2,0:T(8,128)(2,1)}, u32[]{:S(2)}, u32[]{:S(2)}) async-start(bf16[96,256,192]{1,2,0:T(8,128)(2,1)} %gather_fusion.3), calls=%async_computation.1 | async-start | bytes 18874368 | tf_op jit(solution)/shard_map/all_to_all | solution.py:86
  40.9 5.4 gather_fusion.2
  47.1 196.4 %all-to-all-done.1 = bf16[96,256,192]{1,2,0:T(8,128)(2,1)} async-done(((bf16[96,256,192]{1,2,0:T(8,128)(2,1)}), bf16[96,256,192]{1,2,0:T(8,128)(2,1)}, u32[]{:S(2)}, u32[]{:S(2)}) %all-to-all-start.1) | async-done | bytes 9437216 | tf_op jit(solution)/shard_map/all_to_all | solution.py:86
  243.5 7.3 %gather_fusion.4 = bf16[64,256,192]{1,2,0:T(8,128)(2,1)} fusion(bf16[96,256,192]{1,2,0:T(8,128)(2,1)} %all-to-all-done.1, s32[1024]{0:T(1024)S(1)} %pad_clamp_fusion), kind=kCustom, calls=%fused_computation.4 | custom fusion | bytes 12583168 | tf_op jit(solution)/shard_map/gather | solution.py:87
  250.9 40.4 %while.2 = (s32[]{:T(128)}, f32[8,8,256,128]{3,2,1,0:T(8,128)}, f32[8,8,256,128]{3,2,1,0:T(8,128)}, s32[8,8]{1,0:T(8,128)S(1)}, bf16[8,8,256,192]{2,3,1,0:T(8,12...) while((s32[]{:T(128)}, f32[8,8,256,128]{3,2,1,0:T(8,128)}, f32[8,8,256,128]{3,2,1,0:T(8,128)}, ...), condition=%wide.region_4.5_spmd, body=%wide.region_3.4_spmd.sunk | while | flops 337707008 | bytes 10487445 | solution.py:46
  250.9 1.5 dynamic-slice_bitcast_fusion.3
  253.0 1.5 fusion.59
  254.5 1.5 fusion.58
  256.0 1.5 dynamic-slice_bitcast_fusion.3
  258.1 1.5 fusion.59
  261.0 1.5 dynamic-slice_bitcast_fusion.3
  263.1 1.5 fusion.59
  266.0 1.5 dynamic-slice_bitcast_fusion.3
  268.2 1.5 fusion.59
  271.1 1.5 dynamic-slice_bitcast_fusion.3
  273.2 1.5 fusion.59
  274.7 1.5 fusion.58
  276.2 1.5 dynamic-slice_bitcast_fusion.3
  281.2 1.5 dynamic-slice_bitcast_fusion.3
  283.3 1.5 fusion.59
  286.2 1.5 dynamic-slice_bitcast_fusion.3
  288.3 1.5 fusion.59
  291.2 6.0 broadcast_in_dim.37
  297.3 16.1 %scatter_fusion.2 = f32[96,256,128]{2,1,0:T(8,128)} fusion(f32[96,256,128]{2,1,0:T(8,128)} %broadcast_in_dim.37, s32[64]{0:T(128)S(1)} %fusion.30, f32[64,256,128]{2,1,0:T(8,128)} %bitcast.94), kind=kCustom, calls=%fused_computation.8 | custom fusion | bytes 25166080 | tf_op jit(solution)/shard_map/scatter | solution.py:90
  313.4 25.1 %all-to-all-start.2 = ((f32[96,256,128]{2,1,0:T(8,128)}), f32[96,256,128]{2,1,0:T(8,128)}, u32[]{:S(2)}, u32[]{:S(2)}) async-start(f32[96,256,128]{2,1,0:T(8,128)} %scatter_fusion.2), calls=%async_computation.2 | async-start | bytes 25165824 | tf_op jit(solution)/shard_map/all_to_all | solution.py:91
  338.5 1.9 collective-permute-start
  340.4 2.5 gather_fusion
  343.0 32.5 %collective-permute-done = bf16[32,256,192]{1,2,0:T(8,128)(2,1)} collective-permute-done((bf16[32,256,192]{1,2,0:T(8,128)(2,1)}, bf16[32,256,192]{1,2,0:T(8,128)(2,1)}, u32[]{:S(2)}, u32[]{:S(2)}) %collective-permute-start) | collective-permute-done | bytes 3145760 | tf_op jit(solution)/shard_map/ppermute | solution.py:16
  375.5 2.5 gather_fusion.1
  378.6 1.5 fusion.22
  380.1 2.5 broadcast.142
  382.6 3.3 scatter_fusion
  386.0 2.5 convert_element_type.35
  388.5 4.3 collective-permute-start.1
  393.2 23.1 %collective-permute-done.1 = bf16[32,256,128]{2,1,0:T(8,128)(2,1)S(1)} collective-permute-done((bf16[32,256,128]{2,1,0:T(8,128)(2,1)S(1)}, bf16[32,256,128]{2,1,0:T(8,128)(2,1)S(1)}, u32[]{:S(2)}, u32[]{:S(2)}) %collective-permute-start.1) | collective-permute-done | bytes 2097184 | tf_op jit(solution)/shard_map/ppermute | solution.py:16
  416.3 2.5 convert_element_type.36
  418.9 19.1 %scatter_fusion.1 = f32[32,256,128]{2,1,0:T(8,128)} fusion(f32[32,256,128]{2,1,0:T(8,128)} %convert_element_type.36, s32[64]{0:T(128)S(1)} %fusion.29, f32[64,256,128]{2,1,0:T(8,128)} %bitcast.23), kind=kCustom, calls=%fused_computation.7 | custom fusion | flops 2097152 | bytes 25166080 | tf_op jit(solution)/shard_map/scatter-add | solution.py:89
  438.0 181.6 %all-to-all-done.2 = f32[96,256,128]{2,1,0:T(8,128)} async-done(((f32[96,256,128]{2,1,0:T(8,128)}), f32[96,256,128]{2,1,0:T(8,128)}, u32[]{:S(2)}, u32[]{:S(2)}) %all-to-all-start.2) | async-done | bytes 12582944 | tf_op jit(solution)/shard_map/all_to_all | solution.py:91
  619.6 27.8 %scatter_fusion.3 = f32[32,256,128]{2,1,0:T(8,128)} fusion(f32[32,256,128]{2,1,0:T(8,128)} %scatter_fusion.1, s32[96]{0:T(128)S(1)} %fusion.31, f32[96,256,128]{2,1,0:T(8,128)} %all-to-all-done.2), kind=kCustom, calls=%fused_computation.9 | custom fusion | flops 3145728 | bytes 37749120 | tf_op jit(solution)/shard_map/scatter-add | solution.py:92
  647.4 3.3 scatter_fusion.4
  650.8 3.5 multiply_reduce_fusion
  654.4 2.3 fusion.16
  656.7 2.0 fusion.8
  (84 shorter events, 22.3 us)
Async XLA Ops:
  0.0 16.9 %copy-start = (bf16[1,8192,128]{2,1,0:T(8,128)(2,1)S(1)}, bf16[1,8192,128]{2,1,0:T(8,128)(2,1)}, u32[]{:S(2)}) copy-start(bf16[1,8192,128]{2,1,0:T(8,128)(2,1)} %param.16) | copy-start | bytes 6291460
  0.0 16.9 %copy-start.6 = (bf16[128,64]{0,1:T(8,128)(2,1)S(1)}, bf16[128,64]{0,1:T(8,128)(2,1)}, u32[]{:S(2)}) copy-start(bf16[128,64]{0,1:T(8,128)(2,1)} %param.18) | copy-start | bytes 49156
  3.3 18.8 %all-to-all-start = ((s32[32,3,1]{1,2,0:T(1,128)}), s32[32,3,1]{1,2,0:T(1,128)S(1)}, u32[]{:S(2)}, u32[]{:S(2)}) async-start(s32[32,3,1]{1,2,0:T(1,128)} %bitcast.20), calls=%async_computation | async-start | bytes 32768 | tf_op jit(solution)/shard_map/all_to_all | solution.py:84
  32.9 8.0 %copy-start.8 = (s32[1,64]{1,0:T(1,128)S(1)}, s32[1,64]{1,0:T(1,128)}, u32[]{:S(2)}) copy-start(s32[1,64]{1,0:T(1,128)} %param.21) | copy-start | bytes 772
  32.9 210.7 %all-to-all-start.1 = ((bf16[96,256,192]{1,2,0:T(8,128)(2,1)}), bf16[96,256,192]{1,2,0:T(8,128)(2,1)}, u32[]{:S(2)}, u32[]{:S(2)}) async-start(bf16[96,256,192]{1,2,0:T(8,128)(2,1)} %gather_fusion.3), calls=%async_computation.1 | async-start | bytes 18874368 | tf_op jit(solution)/shard_map/all_to_all | solution.py:86
  40.9 5.5 copy-start.9
  313.3 27.1 %copy-start.10 = (s32[1,8]{1,0:T(1,128)S(1)}, s32[1,8]{1,0:T(1,128)}, u32[]{:S(2)}) copy-start(s32[1,8]{1,0:T(1,128)} %param.25) | copy-start | bytes 100
  313.3 29.6 %copy-start.11 = (s32[1,8]{1,0:T(1,128)S(1)}, s32[1,8]{1,0:T(1,128)}, u32[]{:S(2)}) copy-start(s32[1,8]{1,0:T(1,128)} %param.26) | copy-start | bytes 100
  313.4 306.2 %all-to-all-start.2 = ((f32[96,256,128]{2,1,0:T(8,128)}), f32[96,256,128]{2,1,0:T(8,128)}, u32[]{:S(2)}, u32[]{:S(2)}) async-start(f32[96,256,128]{2,1,0:T(8,128)} %scatter_fusion.2), calls=%async_computation.2 | async-start | bytes 25165824 | tf_op jit(solution)/shard_map/all_to_all | solution.py:91
  338.5 39.5 %copy-start.12 = (s32[1,8]{1,0:T(1,128)S(1)}, s32[1,8]{1,0:T(1,128)}, u32[]{:S(2)}) copy-start(s32[1,8]{1,0:T(1,128)} %param.27) | copy-start | bytes 100
  338.5 37.0 %collective-permute-start = (bf16[32,256,192]{1,2,0:T(8,128)(2,1)}, bf16[32,256,192]{1,2,0:T(8,128)(2,1)}, u32[]{:S(2)}, u32[]{:S(2)}) collective-permute-start(bf16[32,256,192]{1,2,0:T(8,128)(2,1)} %bitcast.89), channel_id=1, source_target_pairs={{1,0},{2,1},{3,2},{4,3},{5,4},{6,5},{7,6},{9,8},{10,9},{11,10},{12... | collective-permute-start | bytes 9437192 | tf_op jit(solution)/shard_map/ppermute | solution.py:16
  343.0 35.0 %copy-start.4 = (bf16[8,256,192]{1,2,0:T(8,128)(2,1)}, bf16[8,256,192]{1,2,0:T(8,128)(2,1)S(1)}, u32[]{:S(2)}) copy-start(bf16[8,256,192]{1,2,0:T(8,128)(2,1)S(1)} %gather_fusion) | copy-start | bytes 2359300
  388.5 27.9 %collective-permute-start.1 = (bf16[32,256,128]{2,1,0:T(8,128)(2,1)S(1)}, bf16[32,256,128]{2,1,0:T(8,128)(2,1)S(1)}, u32[]{:S(2)}, u32[]{:S(2)}) collective-permute-start(bf16[32,256,128]{2,1,0:T(8,128)(2,1)S(1)} %convert_element_type.35), channel_id=1, source_target_pairs={{0,1},{1,2},{2,3},{3,4},{4,5},{5,6},{6,7},{8,9},{9,10},{10,11},{11... | collective-permute-start | bytes 6291464 | tf_op jit(solution)/shard_map/ppermute | solution.py:16
  647.4 6.9 %copy-start.7 = (f32[128]{0:T(128)S(1)}, f32[128]{0:T(128)}, u32[]{:S(2)}) copy-start(f32[128]{0:T(128)} %param.20) | copy-start | bytes 1540
  650.8 3.6 copy-start.2
  654.2 2.4 copy-start.3
  654.3 2.4 copy-start.5
  654.3 4.4 copy-start.1
where the time goes:
time: 671 us; the launch traced here: 659 us
  waiting for transfers between devices  436 us (65%)
  local copies, waits for them, and re-layouts  68.3 us (10%)
  other arithmetic  68 us (10%)
  starting transfers between devices  50.6 us (8%)
  matrix products  35.6 us (5%)
    all_to_all x1, waiting for transfers between devices, body(): lax.all_to_all(served, 'space', split_axis=0, concat_axis=0, tiled=True)  196 us
    all_to_all x1, waiting for transfers between devices, body(): lax.all_to_all(returned, 'space', split_axis=0, concat_axis=0, tiled=True)  182 us
    ppermute x2, waiting for transfers between devices, from_behind(): lax.ppermute(value, axis, [(source, source + steps) for source in range(l...  55.6 us
    scatter-add x1, other arithmetic, body(): aggregate = aggregate.at[requested].add(received)  27.8 us
    all_to_all x1, starting transfers between devices, body(): lax.all_to_all(returned, 'space', split_axis=0, concat_axis=0, tiled=True)  25.1 us
    scatter-add x1, other arithmetic, body(): aggregate = aggregate.at[local_ids].add(forward)  19.1 us
    scatter x1, local copies, waits for them, and re-layouts, body(): jnp.zeros((slots, BLK, C), jnp.float32).at[slot_index].set(backward)  16.1 us
    dot_general x9, matrix products, both_terms(): jnp.dot(matrix.T, left_block[:, :C], preferred_element_type=jnp.float32)  13.4 us
  transfers between devices with their start and end apart: 5, of which 5 were waited for; matrix products, arithmetic and copies ran while one was open for 7% of the time, Pallas kernels for 0%

commit v1 on v0

v1 whole, which is shorter than its diff:
```python
import math

import jax
import jax.numpy as jnp
from jax import lax
from jax.experimental import pallas as pl
from jax.experimental.pallas import tpu as pltpu
from jax.sharding import PartitionSpec as P

C = 128
K = 64
BLK = 256
HALF = BLK // 2
ROWS = BLK + HALF
CAP = 3
VMEM_LIMIT = 56 * 1024 * 1024


def group_shift(value, steps):
    count = lax.axis_size("group")
    leading, last = (max(0, -steps), min(count, count - steps))
    return lax.ppermute(value, "group", [(source, source + steps) for source in range(leading, last)])


def plan_slots(t_local, t_dest, t_block, t_cut, spaces):
    pairs = t_local.shape[0]
    slots = spaces * CAP

    def kernel(local_ref, dest_ref, block_ref, cut_ref, used_ref, meta_ref, count):
        @pl.loop(0, slots)
        def _(i):
            used_ref[i] = -1
            meta_ref[2 * i] = 0
            meta_ref[2 * i + 1] = 0

        @pl.loop(0, spaces)
        def _(i):
            count[i] = 0

        @pl.loop(0, pairs)
        def _(t):
            dest = dest_ref[t]
            slot = dest * CAP + count[dest]
            count[dest] = count[dest] + 1
            used_ref[slot] = local_ref[t]
            meta_ref[2 * slot] = block_ref[t]
            meta_ref[2 * slot + 1] = cut_ref[t]

    smem = pl.BlockSpec(memory_space=pltpu.SMEM)
    return pl.pallas_call(
        kernel,
        out_shape=(
            jax.ShapeDtypeStruct((slots,), jnp.int32),
            jax.ShapeDtypeStruct((2 * slots,), jnp.int32),
        ),
        in_specs=[smem] * 4,
        out_specs=(smem, smem),
        scratch_shapes=[pltpu.SMEM((spaces,), jnp.int32)],
        name="plan_slots",
    )(t_local, t_dest, t_block, t_cut)


def project_and_pack(points, geom, w_value, w_kern, used, x_local):
    blocks = points.shape[0] // BLK
    slots = used.shape[0]
    cross = x_local.shape[0]
    step = 4

    def kernel(used_ref, cross_ref, points_ref, geom_ref, wv_ref, wk_ref, own_ref, out_ref, up_ref, held, sems):
        i = pl.program_id(0)
        values = jnp.dot(points_ref[...], wv_ref[...], preferred_element_type=jnp.float32).astype(jnp.bfloat16)
        for b in range(step):
            base = b * BLK
            wide = jnp.concatenate(
                [geom_ref[pl.ds(base, HALF), :], geom_ref[pl.ds(base + HALF, HALF), :]], axis=1
            )
            held[i * step + b, :BLK, :] = values[base : base + BLK]
            held[i * step + b, BLK:, :] = jnp.dot(
                wide, wk_ref[...], preferred_element_type=jnp.float32
            ).astype(jnp.bfloat16)

        @pl.when(i == pl.num_programs(0) - 1)
        def _():
            own = pltpu.make_async_copy(held, own_ref, sems.at[0])

            def cross_copy(t):
                return pltpu.make_async_copy(held.at[cross_ref[t]], up_ref.at[t], sems.at[1])

            def slot_copy(t):
                return pltpu.make_async_copy(held.at[jnp.maximum(used_ref[t], 0)], out_ref.at[t], sems.at[2])

            own.start()
            for t in range(cross):
                cross_copy(t).start()

            @pl.loop(0, slots)
            def _(t):
                slot_copy(t).start()

            own.wait()
            for t in range(cross):
                cross_copy(t).wait()

            @pl.loop(0, slots)
            def _(t):
                slot_copy(t).wait()

    zero = jnp.zeros_like(w_kern)
    twice = jnp.concatenate(
        [jnp.concatenate([w_kern, zero], 1), jnp.concatenate([zero, w_kern], 1)], 0
    )
    anywhere = pl.BlockSpec(memory_space=pl.ANY)
    return pl.pallas_call(
        kernel,
        grid_spec=pltpu.PrefetchScalarGridSpec(
            num_scalar_prefetch=2,
            grid=(blocks // step,),
            in_specs=[
                pl.BlockSpec((step * BLK, C), lambda i, *_: (i, 0)),
                pl.BlockSpec((step * BLK, C), lambda i, *_: (i, 0)),
                pl.BlockSpec((C, C), lambda i, *_: (0, 0)),
                pl.BlockSpec((2 * C, 2 * K), lambda i, *_: (0, 0)),
            ],
            out_specs=(anywhere, anywhere, anywhere),
            scratch_shapes=[
                pltpu.VMEM((blocks, ROWS, C), jnp.bfloat16),
                pltpu.SemaphoreType.DMA((3,)),
            ],
        ),
        out_shape=(
            jax.ShapeDtypeStruct((blocks, ROWS, C), jnp.bfloat16),
            jax.ShapeDtypeStruct((slots, ROWS, C), jnp.bfloat16),
            jax.ShapeDtypeStruct((cross, ROWS, C), jnp.bfloat16),
        ),
        compiler_params=pltpu.CompilerParams(vmem_limit_bytes=VMEM_LIMIT),
        name="project_and_pack",
    )(used, x_local, points, geom, w_value, twice)


def unpack_kernels(packed):
    return jnp.concatenate([packed[:, :K], packed[:, K:]], axis=0)


def pair_terms(theirs, own, cut):
    scores = lax.dot_general(
        unpack_kernels(theirs[BLK:]),
        unpack_kernels(own[BLK:]),
        (((1,), (1,)), ((), ())),
        preferred_element_type=jnp.float32,
    )
    rows = lax.broadcasted_iota(jnp.int32, (BLK, BLK), 0)
    columns = lax.broadcasted_iota(jnp.int32, (BLK, BLK), 1)
    tile = jnp.where(rows + columns < cut, jnp.tanh(scores * (1.0 / math.sqrt(K))), 0.0).astype(jnp.bfloat16)
    forward = jnp.dot(tile, own[:BLK], preferred_element_type=jnp.float32)
    backward = lax.dot_general(
        tile, theirs[:BLK], (((0,), (0,)), ((), ())), preferred_element_type=jnp.float32
    )
    return forward, backward


def pairs(meta, arrived, own, aggregate):
    slots = arrived.shape[0]
    blocks = own.shape[0]
    step = 4

    def kernel(meta_ref, arrived_ref, own_ref, *rest):
        if aggregate is None:
            back_ref, total_ref, total, sem = rest
        else:
            given_ref, back_ref, total_ref, total, sem = rest
        i = pl.program_id(0)

        @pl.when(i == 0)
        def _():
            if aggregate is None:
                total[...] = jnp.zeros_like(total)
            else:
                copy = pltpu.make_async_copy(given_ref, total, sem)
                copy.start()
                copy.wait()

        for b in range(step):
            slot = i * step + b
            mine = meta_ref[2 * slot]
            forward, backward = pair_terms(arrived_ref[b], own_ref[mine], meta_ref[2 * slot + 1])
            back_ref[b] = forward.astype(jnp.bfloat16)
            total[mine] = total[mine] + backward

        @pl.when(i == pl.num_programs(0) - 1)
        def _():
            copy = pltpu.make_async_copy(total, total_ref, sem)
            copy.start()
            copy.wait()

    anywhere = pl.BlockSpec(memory_space=pl.ANY)
    extra = () if aggregate is None else (aggregate,)
    return pl.pallas_call(
        kernel,
        grid_spec=pltpu.PrefetchScalarGridSpec(
            num_scalar_prefetch=1,
            grid=(slots // step,),
            in_specs=[
                pl.BlockSpec((step, ROWS, C), lambda i, *_: (i, 0, 0)),
                pl.BlockSpec((blocks, ROWS, C), lambda i, *_: (0, 0, 0)),
            ]
            + [anywhere] * len(extra),
            out_specs=(pl.BlockSpec((step, BLK, C), lambda i, *_: (i, 0, 0)), anywhere),
            scratch_shapes=[
                pltpu.VMEM((blocks, BLK, C), jnp.float32),
                pltpu.SemaphoreType.DMA,
            ],
        ),
        out_shape=(
            jax.ShapeDtypeStruct((slots, BLK, C), jnp.bfloat16),
            jax.ShapeDtypeStruct((blocks, BLK, C), jnp.float32),
        ),
        compiler_params=pltpu.CompilerParams(vmem_limit_bytes=VMEM_LIMIT),
        cost_estimate=pl.CostEstimate(
            flops=2 * slots * BLK * BLK * (K + 2 * C),
            bytes_accessed=slots * (ROWS + BLK) * C * 2 + blocks * BLK * C * 8,
            transcendentals=slots * BLK * BLK,
        ),
        name="pairs",
    )(meta, arrived, own, *extra)


def gather_and_mix(used, x_local, returned, returned_x, aggregate, points, w_out, gain):
    slots = returned.shape[0]
    cross = returned_x.shape[0]
    blocks = aggregate.shape[0]
    step = 8
    turns = slots // step
    some = 4

    def kernel(used_ref, cross_ref, back_ref, back_x_ref, total_ref, points_ref, w_ref, gain_ref, out_ref, total, sem):
        i = pl.program_id(0)

        @pl.when(i == 0)
        def _():
            copy = pltpu.make_async_copy(total_ref, total, sem)
            copy.start()
            copy.wait()
            for t in range(cross):
                mine = cross_ref[t]
                total[mine] = total[mine] + back_x_ref[t].astype(jnp.float32)

        @pl.when(i < turns)
        def _():
            for b in range(step):
                mine = used_ref[i * step + b]

                @pl.when(mine >= 0)
                def _():
                    total[mine] = total[mine] + back_ref[b].astype(jnp.float32)

        @pl.when(i >= turns)
        def _():
            for b in range(some):
                flat = total[(i - turns) * some + b]
                meansq = jnp.mean(flat * flat, -1, keepdims=True)
                normed = flat * lax.rsqrt(meansq + 1e-06) * gain_ref[...]
                hidden = jax.nn.gelu(normed).astype(jnp.bfloat16)
                mixed = points_ref[pl.ds(b * BLK, BLK), :].astype(jnp.float32) + jnp.dot(
                    hidden, w_ref[...], preferred_element_type=jnp.float32
                )
                out_ref[pl.ds(b * BLK, BLK), :] = mixed.astype(jnp.bfloat16)

    return pl.pallas_call(
        kernel,
        grid_spec=pltpu.PrefetchScalarGridSpec(
            num_scalar_prefetch=2,
            grid=(turns + blocks // some,),
            in_specs=[
                pl.BlockSpec((step, BLK, C), lambda i, *_: (jnp.minimum(i, turns - 1), 0, 0)),
                pl.BlockSpec((cross, BLK, C), lambda i, *_: (0, 0, 0)),
                pl.BlockSpec(memory_space=pl.ANY),
                pl.BlockSpec((some * BLK, C), lambda i, *_: (jnp.maximum(i - turns, 0), 0)),
                pl.BlockSpec((C, C), lambda i, *_: (0, 0)),
                pl.BlockSpec((1, C), lambda i, *_: (0, 0)),
            ],
            out_specs=pl.BlockSpec((some * BLK, C), lambda i, *_: (jnp.maximum(i - turns, 0), 0)),
            scratch_shapes=[
                pltpu.VMEM((blocks, BLK, C), jnp.float32),
                pltpu.SemaphoreType.DMA,
            ],
        ),
        out_shape=jax.ShapeDtypeStruct((blocks * BLK, C), jnp.bfloat16),
        compiler_params=pltpu.CompilerParams(vmem_limit_bytes=VMEM_LIMIT),
        name="gather_and_mix",
    )(used, x_local, returned, returned_x, aggregate, points, w_out, gain[None])


def body(feats, geom, w_value, w_kern, w_out, gain, t_local, t_dest, t_block, t_cut, x_local, x_block, x_cut):
    points = feats[0]
    spaces = lax.axis_size("space")
    used, meta = plan_slots(t_local[0], t_dest[0, :, 0], t_block[0], t_cut[0], spaces)
    meta = lax.all_to_all(meta.reshape(spaces, 2 * CAP), "space", split_axis=0, concat_axis=0, tiled=True)
    meta = meta.reshape(-1)
    cross_meta = group_shift(jnp.stack([x_block[0], x_cut[0]], 1), 1).reshape(-1)
    own, leaving, rising = project_and_pack(points, geom[0], w_value, w_kern, used, x_local[0])
    below = group_shift(rising, 1)
    arrived = lax.all_to_all(leaving, "space", split_axis=0, concat_axis=0, tiled=True)
    back_x, aggregate = pairs(cross_meta, below, own, None)
    returned_x = group_shift(back_x, -1)
    back, aggregate = pairs(meta, arrived, own, aggregate)
    returned = lax.all_to_all(back, "space", split_axis=0, concat_axis=0, tiled=True)
    mixed = gather_and_mix(used, x_local[0], returned, returned_x, aggregate, points, w_out, gain)
    return mixed[None]


def solution(mesh):
    in_specs = (
        P("group", "space", None),
        P("group", "space", None),
        P(),
        P(),
        P(),
        P(),
        P("group", "space"),
        P("group", "space", None),
        P("group", "space"),
        P("group", "space"),
        P("group", "space"),
        P("group", "space"),
        P("group", "space"),
    )
    out_specs = P("group", "space", None)
    return jax.shard_map(body, mesh=mesh, in_specs=in_specs, out_specs=out_specs, check_vma=False)
```

time: 671 us -> 460 us (0.69); the launches traced: 659 us -> 456 us
  waiting for transfers between devices: 436 us -> 323 us
  Pallas kernels: 0 us -> 73.3 us
  other arithmetic: 68 us -> 1.41 us
  local copies, waits for them, and re-layouts: 68.3 us -> 4.96 us
  matrix products: 35.6 us -> 0 us
    pallas_call x0 -> x5, Pallas kernels: none -> 73.3 us  [the longest x2 41.8 us: pairs(): pl.pallas_call(kernel, grid_spec=pltpu.PrefetchScalarGridSpec(num_scalar_...]
    all_to_all x3, waiting for transfers between devices: 380 us -> 308 us  [the longest x1 178 us: body(): lax.all_to_all(leaving, 'space', split_axis=0, concat_axis=0, tiled=True)]
    scatter-add x4 -> x0, other arithmetic: 53.6 us -> none  [the longest x1 27.8 us: body(): aggregate = aggregate.at[requested].add(received)]
    ppermute x2 -> x3, waiting for transfers between devices: 55.6 us -> 14.6 us  [group_shift(): lax.ppermute(value, 'group', [(source, source + steps) for source in rang...]
    dot_general x30 -> x0, matrix products: 35.6 us -> none  [the longest x9 13.4 us: both_terms(): jnp.dot(matrix.T, left_block[:, :C], preferred_element_type=jnp.float32)]
    gather x5 -> x0, local copies, waits for them, and re-layouts: 27.1 us -> none  [the longest x1 9.4 us: body(): served = payload[requested]]
    scatter x2 -> x0, local copies, waits for them, and re-layouts: 17 us -> none  [the longest x1 16.1 us: body(): jnp.zeros((slots, BLK, C), jnp.float32).at[slot_index].set(backward)]
    squeeze x8 -> x0, local copies, waits for them, and re-layouts: 12 us -> none  [blockwise(): result = lax.map(evaluate, shaped)]
  transfers between devices with their start and end apart: 5 -> 6, of which waited for: 5 -> 4; matrix products, arithmetic and copies ran while one was open for 7% -> 1% of each run, Pallas kernels for 0% -> 4%
where the time goes in v1:
time: 460 us; the launch traced here: 456 us
  waiting for transfers between devices  323 us (70%)
  Pallas kernels  73.3 us (16%)
  starting transfers between devices  53.5 us (12%)
  local copies, waits for them, and re-layouts  4.96 us (1%)
    all_to_all x1, waiting for transfers between devices, body(): lax.all_to_all(leaving, 'space', split_axis=0, concat_axis=0, tiled=True)  178 us
    all_to_all x1, waiting for transfers between devices, body(): lax.all_to_all(back, 'space', split_axis=0, concat_axis=0, tiled=True)  130 us
    pallas_call x2, Pallas kernels, pairs(): pl.pallas_call(kernel, grid_spec=pltpu.PrefetchScalarGridSpec(num_scalar_...  41.8 us
    all_to_all x1, starting transfers between devices, body(): lax.all_to_all(back, 'space', split_axis=0, concat_axis=0, tiled=True)  25 us
    pallas_call x1, Pallas kernels, gather_and_mix(): pl.pallas_call(kernel, grid_spec=pltpu.PrefetchScalarGridSpec(num_scalar_...  17.5 us
    ppermute x3, waiting for transfers between devices, group_shift(): lax.ppermute(value, 'group', [(source, source + steps) for source in rang...  14.6 us
    all_to_all x1, starting transfers between devices, body(): lax.all_to_all(meta.reshape(spaces, 2 * CAP), 'space', split_axis=0, conc...  11.2 us
    pallas_call x1, Pallas kernels, project_and_pack(): pl.pallas_call(kernel, grid_spec=pltpu.PrefetchScalarGridSpec(num_scalar_...  11.2 us
  transfers between devices with their start and end apart: 6, of which 4 were waited for; matrix products, arithmetic and copies ran while one was open for 1% of the time, Pallas kernels for 4%

profile of v1, /device:TPU:42, one launch (start us, length us, event | category | flops | bytes accessed | tf_op | source)
XLA Modules:
  0.0 456.3 jit_solution(10696521471535110654)
XLA Ops:
  0.0 2.9 plan_slots.1
  2.9 1.4 all_to_all.12
  4.3 11.2 %all-to-all-start = ((s32[32,1,6]{2,1,0:T(1,128)}), s32[32,1,6]{2,1,0:T(1,128)S(1)}, u32[]{:S(2)}, u32[]{:S(2)}) async-start(s32[32,1,6]{2,1,0:T(1,128)} %bitcast.5), calls=%async_computation | async-start | bytes 32768 | tf_op jit(solution)/shard_map/all_to_all | solution.py:297
  15.5 0.8 copy.21
  16.3 0.7 fusion.2.wk_ref
  17.1 11.2 %project_and_pack.1 = (bf16[32,384,128]{2,1,0:T(8,128)(2,1)}, bf16[96,384,128]{2,1,0:T(8,128)(2,1)}, bf16[8,384,128]{2,1,0:T(8,128)(2,1)}) custom-call(s32[96]{0:T(128)} %get-tuple-element.14.used_ref, s32[8]{0:T(128)} %bitcast.15, bf16[8192,128]{1,0:T(8,128)(2,1)} %bitcast.12, bf16[8192,128]{1,0:T(8,128)(2,1)} %bitcast.14, bf16[128,128]{1,0:T(8,128)(2,1)} %wv_ref.1, ...), custom_call_target="tpu_custom_call" | custom-call | tf_op jit(solution)/shard_map/project_and_pack/pallas_call | solution.py:113
  28.2 0.0 all-to-all-done
  28.2 0.0 copy-start.4
  28.2 0.0 copy-start.2
  28.3 0.0 copy-start.3
  28.3 10.0 %all-to-all-start.1 = ((bf16[96,384,128]{2,1,0:T(8,128)(2,1)}), bf16[96,384,128]{2,1,0:T(8,128)(2,1)}, u32[]{:S(2)}, u32[]{:S(2)}) async-start(bf16[96,384,128]{2,1,0:T(8,128)(2,1)} %get-tuple-element.16), calls=%async_computation.1 | async-start | bytes 18874368 | tf_op jit(solution)/shard_map/all_to_all | solution.py:302
  38.2 0.0 copy-done.4
  38.3 1.9 collective-permute-start.1
  40.2 0.0 copy-done.2
  40.2 0.0 copy-done.3
  40.2 3.5 collective-permute-start
  43.7 7.9 %collective-permute-done = s32[8,2]{0,1:T(2,128)S(1)} collective-permute-done((s32[8,2]{0,1:T(2,128)S(1)}, s32[8,2]{0,1:T(2,128)S(1)}, u32[]{:S(2)}, u32[]{:S(2)}) %collective-permute-start) | collective-permute-done | bytes 96 | tf_op jit(solution)/shard_map/ppermute | solution.py:22
  51.6 0.1 copy.23
  51.7 0.6 reshape.12.meta_ref
  52.3 0.5 broadcast.13
  52.8 0.7 reduce.3
  53.5 0.7 reshape.11.meta_ref
  54.1 0.0 collective-permute-done.1.arrived_ref
  54.2 0.0 copy-start
  54.2 0.9 copy-done
  55.0 7.9 %pairs.2 = (bf16[8,256,128]{2,1,0:T(8,128)(2,1)}, f32[32,256,128]{2,1,0:T(8,128)}) custom-call(s32[16]{0:T(128)} %reshape.12.meta_ref, bf16[8,384,128]{2,1,0:T(8,128)(2,1)} %copy-done, bf16[32,384,128]{2,1,0:T(8,128)(2,1)} %get-tuple-element.17.own_ref), custom_call_target="tpu_custom_call" | custom-call | flops 335544320 | bytes 9699328 | tf_op jit(solution)/shard_map/pairs/pallas_call | solution.py:197
  62.9 178.1 %all-to-all-done.1.arrived_ref = bf16[96,384,128]{2,1,0:T(8,128)(2,1)} async-done(((bf16[96,384,128]{2,1,0:T(8,128)(2,1)}), bf16[96,384,128]{2,1,0:T(8,128)(2,1)}, u32[]{:S(2)}, u32[]{:S(2)}) %all-to-all-start.1) | async-done | bytes 9437216 | tf_op jit(solution)/shard_map/all_to_all | solution.py:302
  241.0 34.0 %pairs.3 = (bf16[96,256,128]{2,1,0:T(8,128)(2,1)}, f32[32,256,128]{2,1,0:T(8,128)}) custom-call(s32[192]{0:T(256)} %reshape.11.meta_ref, bf16[96,384,128]{2,1,0:T(8,128)(2,1)} %all-to-all-done.1.arrived_ref, bf16[32,384,128]{2,1,0:T(8,128)(2,1)} %get-tuple-element.17.own_ref, f32[32,256,128]{2,1,0:T(8,128)} %get-tuple-element.19.rest_0_), custom_call_target="tpu_custom_call" | custom-call | flops 4026531840 | bytes 24117248 | tf_op jit(solution)/shard_map/pairs/pallas_call | solution.py:197
  275.0 0.0 copy-start.5
  275.0 25.0 %all-to-all-start.2 = ((bf16[96,256,128]{2,1,0:T(8,128)(2,1)}), bf16[96,256,128]{2,1,0:T(8,128)(2,1)}, u32[]{:S(2)}, u32[]{:S(2)}) async-start(bf16[96,256,128]{2,1,0:T(8,128)(2,1)} %get-tuple-element.20), calls=%async_computation.2 | async-start | bytes 12582912 | tf_op jit(solution)/shard_map/all_to_all | solution.py:306
  300.0 0.0 copy-done.5
  300.0 1.9 collective-permute-start.2
  301.9 6.7 %collective-permute-done.2.back_x_ref = bf16[8,256,128]{2,1,0:T(8,128)(2,1)S(1)} collective-permute-done((bf16[8,256,128]{2,1,0:T(8,128)(2,1)S(1)}, bf16[8,256,128]{2,1,0:T(8,128)(2,1)S(1)}, u32[]{:S(2)}, u32[]{:S(2)}) %collective-permute-start.2) | collective-permute-done | bytes 524320 | tf_op jit(solution)/shard_map/ppermute | solution.py:22
  308.6 0.0 copy-start.1
  308.6 130.2 %all-to-all-done.2.back_ref = bf16[96,256,128]{2,1,0:T(8,128)(2,1)} async-done(((bf16[96,256,128]{2,1,0:T(8,128)(2,1)}), bf16[96,256,128]{2,1,0:T(8,128)(2,1)}, u32[]{:S(2)}, u32[]{:S(2)}) %all-to-all-start.2) | async-done | bytes 6291488 | tf_op jit(solution)/shard_map/all_to_all | solution.py:306
  438.8 0.0 copy-done.1
  438.8 17.5 %gather_and_mix.1 = bf16[8192,128]{1,0:T(8,128)(2,1)} custom-call(s32[96]{0:T(128)} %get-tuple-element.14.used_ref, s32[8]{0:T(128)} %bitcast.16, bf16[96,256,128]{2,1,0:T(8,128)(2,1)} %all-to-all-done.2.back_ref, bf16[8,256,128]{2,1,0:T(8,128)(2,1)} %copy-done.1, f32[32,256,128]{2,1,0:T(8,128)} %get-tuple-element.22.total_ref, bf16[8192,128]{1,0:T(8,128)(2,1)} %bitcast.13, ...), custom_call_target="tpu_custom_call" | custom-call | tf_op jit(solution)/shard_map/gather_and_mix/pallas_call | solution.py:268
  (1 shorter events, 0.0 us)
Async XLA Ops:
  4.3 24.0 %all-to-all-start = ((s32[32,1,6]{2,1,0:T(1,128)}), s32[32,1,6]{2,1,0:T(1,128)S(1)}, u32[]{:S(2)}, u32[]{:S(2)}) async-start(s32[32,1,6]{2,1,0:T(1,128)} %bitcast.5), calls=%async_computation | async-start | bytes 32768 | tf_op jit(solution)/shard_map/all_to_all | solution.py:297
  28.2 10.0 %copy-start.4 = (bf16[8,384,128]{2,1,0:T(8,128)(2,1)S(1)}, bf16[8,384,128]{2,1,0:T(8,128)(2,1)}, u32[]{:S(2)}) copy-start(bf16[8,384,128]{2,1,0:T(8,128)(2,1)} %get-tuple-element.18) | copy-start | bytes 2359300
  28.2 11.9 %copy-start.2 = (s32[1,8]{1,0:T(1,128)S(1)}, s32[1,8]{1,0:T(1,128)}, u32[]{:S(2)}) copy-start(s32[1,8]{1,0:T(1,128)} %param.25) | copy-start | bytes 100
  28.3 11.9 %copy-start.3 = (s32[1,8]{1,0:T(1,128)S(1)}, s32[1,8]{1,0:T(1,128)}, u32[]{:S(2)}) copy-start(s32[1,8]{1,0:T(1,128)} %param.24) | copy-start | bytes 100
  28.3 212.8 %all-to-all-start.1 = ((bf16[96,384,128]{2,1,0:T(8,128)(2,1)}), bf16[96,384,128]{2,1,0:T(8,128)(2,1)}, u32[]{:S(2)}, u32[]{:S(2)}) async-start(bf16[96,384,128]{2,1,0:T(8,128)(2,1)} %get-tuple-element.16), calls=%async_computation.1 | async-start | bytes 18874368 | tf_op jit(solution)/shard_map/all_to_all | solution.py:302
  38.3 15.9 %collective-permute-start.1 = (bf16[8,384,128]{2,1,0:T(8,128)(2,1)S(1)}, bf16[8,384,128]{2,1,0:T(8,128)(2,1)S(1)}, u32[]{:S(2)}, u32[]{:S(2)}) collective-permute-start(bf16[8,384,128]{2,1,0:T(8,128)(2,1)S(1)} %copy-done.4), channel_id=1, source_target_pairs={{0,1},{1,2},{2,3},{3,4},{4,5},{5,6},{6,7},{8,9},{9,10},{10,11},{11... | collective-permute-start | bytes 2359304 | tf_op jit(solution)/shard_map/ppermute | solution.py:22
  40.2 11.4 %collective-permute-start = (s32[8,2]{0,1:T(2,128)S(1)}, s32[8,2]{0,1:T(2,128)S(1)}, u32[]{:S(2)}, u32[]{:S(2)}) collective-permute-start(s32[8,2]{0,1:T(2,128)S(1)} %pad_add_fusion), channel_id=1, source_target_pairs={{0,1},{1,2},{2,3},{3,4},{4,5},{5,6},{6,7},{8,9},{9,10},{10,11},{11... | collective-permute-start | bytes 200 | tf_op jit(solution)/shard_map/ppermute | solution.py:22
  54.2 0.9 copy-start
  275.0 25.0 %copy-start.5 = (bf16[8,256,128]{2,1,0:T(8,128)(2,1)S(1)}, bf16[8,256,128]{2,1,0:T(8,128)(2,1)}, u32[]{:S(2)}) copy-start(bf16[8,256,128]{2,1,0:T(8,128)(2,1)} %get-tuple-element.21) | copy-start | bytes 1572868
  275.0 163.8 %all-to-all-start.2 = ((bf16[96,256,128]{2,1,0:T(8,128)(2,1)}), bf16[96,256,128]{2,1,0:T(8,128)(2,1)}, u32[]{:S(2)}, u32[]{:S(2)}) async-start(bf16[96,256,128]{2,1,0:T(8,128)(2,1)} %get-tuple-element.20), calls=%async_computation.2 | async-start | bytes 12582912 | tf_op jit(solution)/shard_map/all_to_all | solution.py:306
  300.0 8.6 %collective-permute-start.2 = (bf16[8,256,128]{2,1,0:T(8,128)(2,1)S(1)}, bf16[8,256,128]{2,1,0:T(8,128)(2,1)S(1)}, u32[]{:S(2)}, u32[]{:S(2)}) collective-permute-start(bf16[8,256,128]{2,1,0:T(8,128)(2,1)S(1)} %copy-done.5), channel_id=1, source_target_pairs={{1,0},{2,1},{3,2},{4,3},{5,4},{6,5},{7,6},{9,8},{10,9},{11,10},{12... | collective-permute-start | bytes 1572872 | tf_op jit(solution)/shard_map/ppermute | solution.py:22
  308.6 130.2 %copy-start.1 = (bf16[8,256,128]{2,1,0:T(8,128)(2,1)}, bf16[8,256,128]{2,1,0:T(8,128)(2,1)S(1)}, u32[]{:S(2)}) copy-start(bf16[8,256,128]{2,1,0:T(8,128)(2,1)S(1)} %collective-permute-done.2.back_x_ref) | copy-start | bytes 1572868
